TPU v7x, 32 devices: a whole 2x2x4 slice. The times are simulated.
32 devices in a mesh: runs: 2 (over x), patch: 16 (over z, y, core).
Axes of the slice: x: 2, y: 2, z: 4, core: 2. Of those that a mesh axis runs over, the one named last changes fastest.
Arguments:
- state: float32 [128, 5, 32768], P(('runs', 'patch')), parts along dimension 0, may hold values from -1 to 6, as said below
- levels: int32 [128], P(('runs', 'patch')), parts along dimension 0, may hold values from 0 to 1
- neighbors: int32 [6, 128], P(None, ('runs', 'patch')), parts along dimension 1, may hold values from -1 to 63, as said below
- new_counts: int32 [32], P(('runs', 'patch')), parts along dimension 0, may hold values from 2 to 6, as said below
Outputs:
- advanced: float32 [192, 5, 32768], P(('runs', 'patch')), parts along dimension 0
- gravity: float32 [3, 128], P(None, ('runs', 'patch')), parts along dimension 1
There are 2 independent parts, one for each index of `runs`. A program takes and returns all parts, laid end to end along the dimension named above; each array names one. Nothing has to cross between parts.
Inputs may be any that keep to these rules, and one draw needn't show every extreme that they name: `state`: field 0 is density, fields 1 to 3 momentum, field 4 total energy; density and pressure 0.4 (E - |m|^2 / (2 rho)) lie in 0.5 to 2 and every velocity component in -0.5 to 0.5. `neighbors`: -1 marks a face on the domain's boundary; any other entry is a curve position less than the patch's own for low faces and greater for high faces, at most 2 away. `new_counts`: the entries sum to 64; for every device d the sum of the entries before d differs from d * 4 by at most 1; some device receives 3 * 2 positions.
All inputs are finite; a program needn't handle non-finite values.
Results may differ from a plain program's by a relative error of at most 0.0003.
Values sent between devices are 32-bit elements; how exact they have to be, the bound alone decides.
A program may use at most 128 MiB of HBM per device.

v0:
```python
import jax
import jax.numpy as jnp
from jax import lax
from jax.sharding import PartitionSpec as P

FIELDS = 5
EDGE = 32
CAP = 6


GAMMA = 1.4
DT_STEP = 0.01
GRAV_C = 2.0
SOFTEN = 0.25


def extended_2(x, sides, width):
    for axis, dim in sides:
        size, length = (lax.axis_size(axis), x.shape[dim])
        up = [(i, (i + 1) % size) for i in range(size - 1)]
        down = [(j, i) for i, j in up]
        last = lax.slice_in_dim(x, length - width, length, axis=dim)
        first = lax.slice_in_dim(x, 0, width, axis=dim)
        before = lax.ppermute(last, axis, up)
        after = lax.ppermute(first, axis, down)
        x = jnp.concatenate([before, x, after], axis=dim)
    return x


def flux_speed(conserved, direction):
    density = conserved[:, 0]
    moment = conserved[:, direction + 1]
    velocity = moment / density
    kinetic = (
        0.5
        * (
            conserved[:, 1] * conserved[:, 1]
            + conserved[:, 2] * conserved[:, 2]
            + conserved[:, 3] * conserved[:, 3]
        )
        / density
    )
    pressure = (GAMMA - 1.0) * (conserved[:, 4] - kinetic)
    sound_speed = jnp.sqrt(GAMMA * pressure / density)
    pieces = [moment]
    for component in range(3):
        summand = conserved[:, component + 1] * velocity
        if component == direction:
            summand = summand + pressure
        pieces.append(summand)
    pieces.append((conserved[:, 4] + pressure) * velocity)
    return (jnp.stack(pieces, axis=1), jnp.abs(velocity) + sound_speed)


def rusanov(lower_state, upper_state, direction):
    flux_lower, speed_lower = flux_speed(lower_state, direction)
    flux_upper, speed_upper = flux_speed(upper_state, direction)
    wave_speed = jnp.maximum(speed_lower, speed_upper)
    return 0.5 * (flux_lower + flux_upper) - 0.5 * wave_speed[:, None] * (upper_state - lower_state)


def face_layers(fields_now):
    patch_count, field_count, edge_cells, plane_cells = fields_now.shape
    cube_view = fields_now.reshape(patch_count, field_count, edge_cells, edge_cells, edge_cells)
    layers = [
        fields_now[:, :, 0],
        fields_now[:, :, edge_cells - 1],
        cube_view[:, :, :, 0].reshape(patch_count, field_count, plane_cells),
        cube_view[:, :, :, edge_cells - 1].reshape(patch_count, field_count, plane_cells),
        cube_view[:, :, :, :, 0].reshape(patch_count, field_count, plane_cells),
        cube_view[:, :, :, :, edge_cells - 1].reshape(patch_count, field_count, plane_cells),
    ]
    return jnp.stack(layers, axis=1)


def collect(buffer, face_data, neighbor_ids, slot_index):
    ghosts = []
    for face_number in range(6):
        chosen = buffer[slot_index[face_number], face_number ^ 1]
        present = neighbor_ids[face_number] >= 0
        ghosts.append(jnp.where(present[:, None, None], chosen, face_data[:, face_number]))
    return ghosts


def euler_update(fields_now, face_data, ghosts, step_ratio, accel):
    patch_count, field_count, edge_cells, plane_cells = fields_now.shape
    column = lax.broadcasted_iota(jnp.int32, (plane_cells,), 0)
    row_y = column // edge_cells
    row_z = column % edge_cells

    def spread_y(face_layer):
        return jnp.tile(
            face_layer.reshape(patch_count, field_count, edge_cells, edge_cells),
            (1, 1, 1, edge_cells),
        )

    def spread_z(face_layer):
        return jnp.repeat(
            face_layer.reshape(patch_count, field_count, edge_cells, edge_cells), edge_cells, axis=3
        )

    below_x = jnp.concatenate([ghosts[0][:, :, None], fields_now[:, :, :-1]], axis=2)
    lower_x = rusanov(below_x, fields_now, 0)
    edge_x = rusanov(face_data[:, 1], ghosts[1], 0)
    upper_x = jnp.concatenate([lower_x[:, :, 1:], edge_x[:, :, None]], axis=2)
    below_y = jnp.where(row_y == 0, spread_y(ghosts[2]), jnp.roll(fields_now, edge_cells, axis=3))
    lower_y = rusanov(below_y, fields_now, 1)
    edge_y = rusanov(face_data[:, 3], ghosts[3], 1)
    upper_y = jnp.where(
        row_y == edge_cells - 1, spread_y(edge_y), jnp.roll(lower_y, -edge_cells, axis=3)
    )
    below_z = jnp.where(row_z == 0, spread_z(ghosts[4]), jnp.roll(fields_now, 1, axis=3))
    lower_z = rusanov(below_z, fields_now, 2)
    edge_z = rusanov(face_data[:, 5], ghosts[5], 2)
    upper_z = jnp.where(row_z == edge_cells - 1, spread_z(edge_z), jnp.roll(lower_z, -1, axis=3))
    divergence = upper_x - lower_x + (upper_y - lower_y) + (upper_z - lower_z)
    density = fields_now[:, 0]
    pull_x = accel[0][:, None, None]
    pull_y = accel[1][:, None, None]
    pull_z = accel[2][:, None, None]
    source = jnp.stack(
        [
            jnp.zeros_like(density),
            density * pull_x,
            density * pull_y,
            density * pull_z,
            fields_now[:, 1] * pull_x + fields_now[:, 2] * pull_y + fields_now[:, 3] * pull_z,
        ],
        axis=1,
    )
    return fields_now - step_ratio[:, None, None, None] * divergence + DT_STEP * source


def curve_coords(positions, total_bits):
    coords = [jnp.zeros_like(positions), jnp.zeros_like(positions), jnp.zeros_like(positions)]
    for bit_index in range(total_bits):
        bit_value = positions // 2**bit_index % 2
        coords[bit_index % 3] = coords[bit_index % 3] + bit_value * 2 ** (bit_index // 3)
    return [
        coords[0].astype(jnp.float32) + 0.5,
        coords[1].astype(jnp.float32) + 0.5,
        coords[2].astype(jnp.float32) + 0.5,
    ]


def gravity_at(positions, masses, npatch):
    total_bits = npatch.bit_length() - 1
    target = curve_coords(positions, total_bits)
    sources = curve_coords(jnp.arange(npatch, dtype=jnp.int32), total_bits)
    offsets = [
        sources[axis_number][None, :] - target[axis_number][:, None] for axis_number in range(3)
    ]
    distance = offsets[0] * offsets[0] + offsets[1] * offsets[1] + offsets[2] * offsets[2] + SOFTEN
    weight = masses[None, :] / (distance * jnp.sqrt(distance))
    strength = GRAV_C / float(npatch) ** (1.0 / 3.0)
    return jnp.stack(
        [strength * jnp.sum(weight * offsets[axis_number], axis=1) for axis_number in range(3)],
        axis=0,
    )


def patch_mass(state, levels):
    return jnp.mean(state[:, 0, :], axis=1) * jnp.exp2(-3.0 * levels.astype(jnp.float32))


def ratio_of(levels):
    return 0.025 * jnp.exp2(levels.astype(jnp.float32))


def ghost_buffer(face_data, live_count, window):
    leading = face_data[:window]
    trailing = lax.dynamic_slice_in_dim(face_data, live_count - window, window, 0)
    edge_rows = jnp.concatenate([leading, trailing], axis=0)
    extended = extended_2(edge_rows, (("patch", 0),), window)
    lower_rows = extended[:window]
    upper_rows = extended[3 * window :]
    return jnp.concatenate([lower_rows, face_data, upper_rows], axis=0)


def local_index(neighbor_ids, live_start, live_count, window, held_rows):
    shifted = window + neighbor_ids - live_start
    beyond = neighbor_ids >= live_start + live_count
    slot_index = jnp.where(beyond, shifted + held_rows - live_count, shifted)
    return jnp.clip(slot_index, 0, held_rows + 2 * window - 1)


def update_each(shaped, face_data, ghosts, step_ratio, accel):
    stacked = jnp.stack(ghosts, axis=1)

    def update_one(items):
        cells, faces, ghost_set, ratio_one, pull = items
        ghost_list = [ghost_set[None, face_number] for face_number in range(6)]
        return euler_update(cells[None], faces[None], ghost_list, ratio_one[None], pull[:, None])[0]

    return lax.map(update_one, (shaped, face_data, stacked, step_ratio, jnp.transpose(accel)))


def run_section(fields_all, neighbor_ids, step_ratio, accel, live_start, live_count, window):
    held_rows = fields_all.shape[0]
    shaped = fields_all.reshape(held_rows, FIELDS, EDGE, EDGE * EDGE)
    face_data = face_layers(shaped)
    buffer = ghost_buffer(face_data, live_count, window)
    slot_index = local_index(neighbor_ids, live_start, live_count, window, held_rows)
    ghosts = collect(buffer, face_data, neighbor_ids, slot_index)
    return update_each(shaped, face_data, ghosts, step_ratio, accel).reshape(fields_all.shape)


def advance_rk(fields_all, neighbor_ids, step_ratio, accel, live_start, live_count, window):
    section_one = run_section(
        fields_all, neighbor_ids, step_ratio, accel, live_start, live_count, window
    )
    return 0.5 * fields_all + 0.5 * run_section(
        section_one, neighbor_ids, step_ratio, accel, live_start, live_count, window
    )


def relocate(rows_now, new_start, new_count):
    held_rows = rows_now.shape[0]
    extended = extended_2(rows_now, (("patch", 0),), held_rows)
    anchor = lax.axis_index("patch") * held_rows
    filler = jnp.zeros((CAP,) + rows_now.shape[1:], rows_now.dtype)
    padded = jnp.concatenate([extended, filler], axis=0)
    taken = lax.dynamic_slice_in_dim(padded, new_start - anchor + held_rows, CAP, 0)
    occupied = lax.broadcasted_iota(jnp.int32, (CAP,), 0) < new_count
    return (taken, occupied)


def local(state, levels, neighbors, new_counts):
    held_rows = state.shape[0]
    devices = lax.axis_size("patch")
    npatch = held_rows * devices
    window = held_rows // 2
    device_rank = lax.axis_index("patch")
    every_count = lax.all_gather(new_counts, "patch", axis=0, tiled=True)
    device_ids = jnp.arange(devices, dtype=jnp.int32)
    new_count = jnp.sum(jnp.where(device_ids == device_rank, every_count, 0))
    new_start = jnp.sum(jnp.where(device_ids < device_rank, every_count, 0))
    masses = patch_mass(state, levels)
    all_masses = lax.all_gather(masses, "patch", axis=0, tiled=True)
    old_start = device_rank * held_rows
    old_positions = old_start + jnp.arange(held_rows, dtype=jnp.int32)
    gravity_old = gravity_at(old_positions, all_masses, npatch)
    result = advance_rk(
        state, neighbors, ratio_of(levels), gravity_old, old_start, held_rows, window
    )
    arrived, occupied = relocate(result, new_start, new_count)
    advanced = jnp.where(occupied[:, None, None], arrived, jnp.zeros_like(arrived))
    return (advanced, gravity_old)


def solution(mesh):
    return jax.shard_map(
        local,
        mesh=mesh,
        in_specs=(
            P(("runs", "patch"), None, None),
            P(("runs", "patch")),
            P(None, ("runs", "patch")),
            P(("runs", "patch")),
        ),
        out_specs=(P(("runs", "patch"), None, None), P(None, ("runs", "patch"))),
        check_vma=False,
    )
```

profile of v0, /device:TPU:0, one launch (start us, length us, event | category | flops | bytes accessed | tf_op | source)
XLA Modules:
  0.0 711.2 jit_solution(132348327442883098)
XLA Ops:
  0.6 3.4 reshape.5104
  4.0 7.8 %reshape_reshape.3 = f32[4,5,32,32,32]{4,3,2,0,1:T(8,128)} reshape(f32[4,5,32768]{2,0,1:T(4,128)} %param.8) | data formatting | bytes 5242880 | tf_op jit(solution)/shard_map/reshape;reshape | solution.py:64
  11.8 3.9 fusion.155
  15.8 12.8 %slice_reduce_fusion.10 = (f32[4,5,32,32]{3,2,0,1:T(8,128)}, f32[4,5,32,32]{3,2,0,1:T(8,128)}) fusion(f32[4,5,32,32,32]{4,3,2,0,1:T(8,128)} %reshape_reshape.3), kind=kLoop, calls=%fused_computation.397 | loop fusion | bytes 327680 | tf_op jit(solution)/shard_map/slice | solution.py:71
  43.9 35.7 %all-reduce.7 = f32[64]{0:T(128)S(1)} all-reduce(f32[64]{0:T(128)S(1)} %get-tuple-element.578), channel_id=1, replica_groups=mesh['runs'=2,'patch'=16] {'patch'}, use_global_device_ids=true, to_apply=%add.7 | all-reduce | flops 64 | bytes 512
  104.3 229.2 %while.26 = (s32[]{:T(128)}, f32[4,5,32,1024]{3,2,1,0:T(8,128)S(1)}, f32[4,5,32,1024]{3,2,0,1:T(8,128)}, f32[4]{0:T(128)}, f32[4,6,5,1024]{3,0,2,1:T(4,128)}, /*...) while((s32[]{:T(128)}, ...), condition=%wide.region_6.7_spmd, body=%wide.region_5.6_spmd.sunk | while | flops 10155010 | bytes 97376112 | solution.py:195
  151.6 3.4 tile.50
  157.9 4.0 fusion.174
  208.8 3.4 tile.50
  215.1 4.0 fusion.174
  266.0 3.4 tile.50
  272.2 4.0 fusion.174
  323.2 3.4 tile.50
  329.4 4.0 fusion.174
  333.5 6.3 reshape_reshape_reshape.3
  339.8 3.6 copy.132
  343.5 5.1 slice_reduce_fusion.13
  348.6 12.8 %slice_reduce_fusion.8 = (f32[4,5,32,32]{3,2,1,0:T(8,128)}, f32[4,5,32,32]{3,2,1,0:T(8,128)}) fusion(f32[4,5,32,32,32]{4,3,2,1,0:T(8,128)} %reshape_reshape_reshape.3), kind=kLoop, calls=%fused_computation.395 | loop fusion | bytes 327680 | tf_op jit(solution)/shard_map/slice | solution.py:71
  401.4 223.3 %while.27 = (s32[]{:T(128)}, f32[4,5,32,1024]{3,2,0,1:T(8,128)}, f32[4,5,32,1024]{3,2,1,0:T(8,128)S(1)}, f32[4]{0:T(128)S(1)}, f32[4,6,5,1024]{3,0,2,1:T(4,128)}...) while((s32[]{:T(128)}, f32[4,5,32,1024]{3,2,0,1:T(8,128)}, ...), condition=%wide.region_8.9_spmd, body=%wide.region_7.8_spmd.sunk | while | flops 9860100 | bytes 78241384 | solution.py:195
  422.5 3.4 tile.53
  452.7 4.7 fusion.179
  478.3 3.4 tile.53
  508.4 4.7 fusion.179
  534.0 3.4 tile.53
  564.2 4.7 fusion.179
  589.8 3.4 tile.53
  619.9 4.8 fusion.179
  624.7 4.9 reshape.5105
  629.6 4.1 add_multiply_fusion
  633.7 4.6 collective-permute-start.4
  641.0 58.7 %all-reduce.6 = s32[16]{0:T(128)S(1)} all-reduce(s32[16]{0:T(128)S(1)} %dynamic-update-slice), channel_id=1, replica_groups=mesh['runs'=2,'patch'=16] {'patch'}, use_global_device_ids=true, to_apply=%add.6 | all-reduce | flops 16 | bytes 128
  702.6 8.1 %fusion.62 = f32[6,5,32768]{2,0,1:T(8,128)} fusion(f32[6,5,32768]{2,0,1:T(8,128)S(1)} %broadcast.2252, s32[]{:T(128)S(6)} %select_n.592, f32[4,5,32768]{2,0,1:T(4,128)S(1)} %collective-permute-done.4, f32[4,5,32768]{2,0,1:T(4,128)} %add_multiply_fusion, f32[4,5,32768]{2,0,1:T(4,128)} %collective-permute-done.5, pred[6]{0:T(512)(128)(4,1)S(1)} %iota_compare_fusion), kind=kLoop, calls=%fused_computation.402 | loop fusion | flops 3932160 | bytes 15728650 | tf_op jit(solution)/shard_map/jit(_where)/select_n | solution.py:247
  (1478 shorter events, 468.4 us)
Async XLA Ops:
  4.0 24.6 %copy-start.11 = (f32[4,5,32,1024]{3,2,0,1:T(8,128)}, f32[4,5,32,1024]{3,2,0,1:T(8,128)S(1)}, u32[]{:S(2)}) copy-start(f32[4,5,32,1024]{3,2,0,1:T(8,128)S(1)} %reshape.5104) | copy-start | bytes 7864324
  28.7 13.2 %copy-start.87 = (u32[32]{0:T(128)S(1)}, u32[32]{0:T(128)}, u32[]{:S(2)}) copy-start(u32[32]{0:T(128)} %constant.657) | copy-start | bytes 388
  28.8 14.5 %copy-start.84 = (s32[4]{0:T(128)S(1)}, s32[4]{0:T(128)}, u32[]{:S(2)}) copy-start(s32[4]{0:T(128)} %param.9) | copy-start | bytes 52
  30.6 49.4 %copy-start.62 = (f32[4,1,5,1024]{3,0,2,1:T(4,128)}, f32[4,1,5,1024]{3,0,2,1:T(4,128)S(1)}, u32[]{:S(2)}) copy-start(f32[4,1,5,1024]{3,0,2,1:T(4,128)S(1)} %stack_reshape_squeeze.24) | copy-start | bytes 245764
  31.8 48.2 %copy-start.60 = (f32[4,1,5,1024]{3,0,2,1:T(4,128)}, f32[4,1,5,1024]{3,0,2,1:T(4,128)S(1)}, u32[]{:S(2)}) copy-start(f32[4,1,5,1024]{3,0,2,1:T(4,128)S(1)} %stack_reshape_squeeze.25) | copy-start | bytes 245764
  33.0 47.1 %copy-start.58 = (f32[4,1,5,1024]{3,0,2,1:T(4,128)}, f32[4,1,5,1024]{3,0,2,1:T(4,128)S(1)}, u32[]{:S(2)}) copy-start(f32[4,1,5,1024]{3,0,2,1:T(4,128)S(1)} %stack_reshape_squeeze.26) | copy-start | bytes 245764
  34.1 45.9 %copy-start.56 = (f32[4,1,5,1024]{3,0,2,1:T(4,128)}, f32[4,1,5,1024]{3,0,2,1:T(4,128)S(1)}, u32[]{:S(2)}) copy-start(f32[4,1,5,1024]{3,0,2,1:T(4,128)S(1)} %stack_reshape_squeeze.27) | copy-start | bytes 245764
  35.4 46.5 %collective-permute-start = (f32[2,6,5,1024]{3,2,0,1:T(8,128)}, f32[2,6,5,1024]{3,2,0,1:T(8,128)}, u32[]{:S(2)}, u32[]{:S(2)}) collective-permute-start(f32[2,6,5,1024]{3,2,0,1:T(8,128)} %get-tuple-element.576), channel_id=1, source_target_pairs={{0,1},{1,2},{2,3},{3,4},{4,5},{5,6},{6,7},{7,8},{8,9},{9,10},{10,1... | collective-permute-start | bytes 737288 | tf_op jit(solution)/shard_map/ppermute | solution.py:24
  38.5 43.4 %collective-permute-start.1 = (f32[2,6,5,1024]{3,2,0,1:T(8,128)}, f32[2,6,5,1024]{3,2,0,1:T(8,128)}, u32[]{:S(2)}, u32[]{:S(2)}) collective-permute-start(f32[2,6,5,1024]{3,2,0,1:T(8,128)} %get-tuple-element.577), channel_id=1, source_target_pairs={{1,0},{2,1},{3,2},{4,3},{5,4},{6,5},{7,6},{8,7},{9,8},{10,9},{11,1... | collective-permute-start | bytes 737288 | tf_op jit(solution)/shard_map/ppermute | solution.py:25
  40.1 58.8 %copy-start.77 = (pred[4]{0:T(512)(128)(4,1)}, pred[4]{0:T(512)(128)(4,1)S(1)}, u32[]{:S(2)}) copy-start(pred[4]{0:T(512)(128)(4,1)S(1)} %get-tuple-element.383) | copy-start | bytes 16
  40.1 59.8 %copy-start.76 = (pred[4]{0:T(512)(128)(4,1)}, pred[4]{0:T(512)(128)(4,1)S(1)}, u32[]{:S(2)}) copy-start(pred[4]{0:T(512)(128)(4,1)S(1)} %get-tuple-element.382) | copy-start | bytes 16
  40.1 60.8 %copy-start.75 = (pred[4]{0:T(512)(128)(4,1)}, pred[4]{0:T(512)(128)(4,1)S(1)}, u32[]{:S(2)}) copy-start(pred[4]{0:T(512)(128)(4,1)S(1)} %get-tuple-element.381) | copy-start | bytes 16
  40.1 61.8 %copy-start.74 = (pred[4]{0:T(512)(128)(4,1)}, pred[4]{0:T(512)(128)(4,1)S(1)}, u32[]{:S(2)}) copy-start(pred[4]{0:T(512)(128)(4,1)S(1)} %get-tuple-element.380) | copy-start | bytes 16
  40.1 62.8 %copy-start.73 = (pred[4]{0:T(512)(128)(4,1)}, pred[4]{0:T(512)(128)(4,1)S(1)}, u32[]{:S(2)}) copy-start(pred[4]{0:T(512)(128)(4,1)S(1)} %get-tuple-element.384) | copy-start | bytes 16
  40.1 62.9 %copy-start.72 = (pred[4]{0:T(512)(128)(4,1)}, pred[4]{0:T(512)(128)(4,1)S(1)}, u32[]{:S(2)}) copy-start(pred[4]{0:T(512)(128)(4,1)S(1)} %get-tuple-element.379) | copy-start | bytes 16
  81.8 15.0 %copy-start.69 = (s32[4]{0:T(128)}, s32[4]{0:T(128)S(1)}, u32[]{:S(2)}) copy-start(s32[4]{0:T(128)S(1)} %get-tuple-element.587) | copy-start | bytes 52
  83.2 15.7 %copy-start.55 = (f32[4,5,1,1024]{3,2,0,1:T(1,128)S(1)}, f32[4,5,1,1024]{3,2,0,1:T(1,128)}, u32[]{:S(2)}) copy-start(f32[4,5,1,1024]{3,2,0,1:T(1,128)} %copy-done.54) | copy-start | bytes 245764
  83.2 17.7 %copy-start.63 = (f32[4,1,5,1024]{3,0,2,1:T(4,128)S(1)}, f32[4,1,5,1024]{3,0,2,1:T(4,128)}, u32[]{:S(2)}) copy-start(f32[4,1,5,1024]{3,0,2,1:T(4,128)} %copy-done.62) | copy-start | bytes 245764
  83.2 18.7 %copy-start.61 = (f32[4,1,5,1024]{3,0,2,1:T(4,128)S(1)}, f32[4,1,5,1024]{3,0,2,1:T(4,128)}, u32[]{:S(2)}) copy-start(f32[4,1,5,1024]{3,0,2,1:T(4,128)} %copy-done.60) | copy-start | bytes 245764
  83.2 19.7 %copy-start.59 = (f32[4,1,5,1024]{3,0,2,1:T(4,128)S(1)}, f32[4,1,5,1024]{3,0,2,1:T(4,128)}, u32[]{:S(2)}) copy-start(f32[4,1,5,1024]{3,0,2,1:T(4,128)} %copy-done.58) | copy-start | bytes 245764
  83.2 19.8 %copy-start.57 = (f32[4,1,5,1024]{3,0,2,1:T(4,128)S(1)}, f32[4,1,5,1024]{3,0,2,1:T(4,128)}, u32[]{:S(2)}) copy-start(f32[4,1,5,1024]{3,0,2,1:T(4,128)} %copy-done.56) | copy-start | bytes 245764
  372.5 4.5 collective-permute-start.2
  374.5 3.9 collective-permute-start.3
  379.8 17.3 %copy-start.52 = (f32[4,1,5,1024]{3,2,0,1:T(8,128)S(1)}, f32[4,1,5,1024]{3,2,0,1:T(8,128)}, u32[]{:S(2)}) copy-start(f32[4,1,5,1024]{3,2,0,1:T(8,128)} %reshape.5342) | copy-start | bytes 245764
  379.8 18.3 %copy-start.53 = (f32[4,1,5,1024]{3,2,0,1:T(8,128)S(1)}, f32[4,1,5,1024]{3,2,0,1:T(8,128)}, u32[]{:S(2)}) copy-start(f32[4,1,5,1024]{3,2,0,1:T(8,128)} %reshape.5343) | copy-start | bytes 245764
  379.8 19.0 %copy-start.51 = (f32[4,1,5,1024]{3,2,0,1:T(8,128)S(1)}, f32[4,1,5,1024]{3,2,0,1:T(8,128)}, u32[]{:S(2)}) copy-start(f32[4,1,5,1024]{3,2,0,1:T(8,128)} %reshape.5344) | copy-start | bytes 245764
  383.7 17.8 %copy-start.86 = (f32[4]{0:T(128)S(1)}, f32[4]{0:T(128)}, u32[]{:S(2)}) copy-start(f32[4]{0:T(128)} %get-tuple-element.1121) | copy-start | bytes 52
  629.6 72.0 %copy-start.79 = (f32[1,4]{1,0:T(1,128)S(1)}, f32[1,4]{1,0:T(1,128)}, u32[]{:S(2)}) copy-start(f32[1,4]{1,0:T(1,128)} %copy-done.78) | copy-start | bytes 52
  629.6 72.0 %copy-start.81 = (f32[1,4]{1,0:T(1,128)S(1)}, f32[1,4]{1,0:T(1,128)}, u32[]{:S(2)}) copy-start(f32[1,4]{1,0:T(1,128)} %copy-done.80) | copy-start | bytes 52
  629.6 72.0 %copy-start.83 = (f32[1,4]{1,0:T(1,128)S(1)}, f32[1,4]{1,0:T(1,128)}, u32[]{:S(2)}) copy-start(f32[1,4]{1,0:T(1,128)} %copy-done.82) | copy-start | bytes 52
  633.7 68.5 %collective-permute-start.4 = (f32[4,5,32768]{2,0,1:T(4,128)}, f32[4,5,32768]{2,0,1:T(4,128)S(1)}, u32[]{:S(2)}, u32[]{:S(2)}) collective-permute-start(f32[4,5,32768]{2,0,1:T(4,128)} %add_multiply_fusion), channel_id=1, source_target_pairs={{0,1},{1,2},{2,3},{3,4},{4,5},{5,6},{6,7},{7,8},{8,9},{9,10},{10,1... | collective-permute-start | bytes 7864328 | tf_op jit(solution)/shard_map/ppermute | solution.py:24
  638.3 63.9 %collective-permute-start.5 = (f32[4,5,32768]{2,0,1:T(4,128)}, f32[4,5,32768]{2,0,1:T(4,128)}, u32[]{:S(2)}, u32[]{:S(2)}) collective-permute-start(f32[4,5,32768]{2,0,1:T(4,128)} %add_multiply_fusion), channel_id=1, source_target_pairs={{1,0},{2,1},{3,2},{4,3},{5,4},{6,5},{7,6},{8,7},{9,8},{10,9},{11,1... | collective-permute-start | bytes 7864328 | tf_op jit(solution)/shard_map/ppermute | solution.py:25
  (212 other events, 732.9 us)
where the time goes:
time: 724 us; the launch traced here: 711 us
  local copies, waits for them, and re-layouts  396 us (55%)
  other arithmetic  197 us (27%)
  blocking collectives  94.4 us (13%)
  starting transfers between devices  13.6 us (2%)
    another operation x40, local copies, waits for them, and re-layouts, spread_y(): jnp.tile(face_layer.reshape(patch_count, field_count, edge_cells, edge_ce...  99.5 us
    unnamed x2, blocking collectives  94.4 us
    broadcast_in_dim x32, local copies, waits for them, and re-layouts, spread_z(): jnp.repeat(face_layer.reshape(patch_count, field_count, edge_cells, edge_...  84.5 us
    dynamic_update_slice x8, other arithmetic, update_each(): lax.map(update_one, (shaped, face_data, stacked, step_ratio, jnp.transpos...  35 us
    while x180, other arithmetic  31.7 us
    gather x12, local copies, waits for them, and re-layouts, collect(): chosen = buffer[slot_index[face_number], face_number ^ 1]  28.2 us
    slice x2, local copies, waits for them, and re-layouts, face_layers(): cube_view[:, :, :, :, edge_cells - 1]  25.7 us
    sub x8, other arithmetic, rusanov(): upper_state - lower_state  21.4 us
  transfers between devices with their start and end apart: 6, of which 1 were waited for; matrix products, arithmetic and copies ran while one was open for 1% of the time, Pallas kernels for 0%

commit v1 on v0

v1 whole, which is shorter than its diff:
```python
import jax
import jax.numpy as jnp
from jax import lax
from jax.experimental import pallas as pl
from jax.experimental.pallas import tpu as pltpu
from jax.sharding import PartitionSpec as P

FIELDS = 5
EDGE = 32
CAP = 6
LANES = 128
ROWS = 8
PLANES = 32
TILES = 256

GAMMA = 1.4
DT_STEP = 0.01
GRAV_C = 2.0
SOFTEN = 0.25
UNROLL = 4


def primitives(u):
    density, m1, m2, m3, energy = u
    inverse = pl.reciprocal(density, approx=True)
    inverse = inverse * (2.0 - density * inverse)
    velocity = [m1 * inverse, m2 * inverse, m3 * inverse]
    twice_kinetic = m1 * velocity[0] + m2 * velocity[1] + m3 * velocity[2]
    pressure = (GAMMA - 1.0) * energy - (0.5 * (GAMMA - 1.0)) * twice_kinetic
    square = GAMMA * pressure * inverse
    sound = square * lax.rsqrt(jnp.maximum(square, 1e-30))
    return velocity, pressure, sound, energy + pressure


def flux(u, prim, k):
    velocity, pressure, sound, enthalpy = prim
    speed = velocity[k]
    out = [u[k + 1]]
    for c in range(3):
        term = u[c + 1] * speed
        out.append(term + pressure if c == k else term)
    out.append(enthalpy * speed)
    return out, jnp.abs(speed) + sound


def interface(lower, upper):
    u_l, f_l, s_l = lower
    u_r, f_r, s_r = upper
    wave = jnp.maximum(s_l, s_r)
    return [(f_l[i] + f_r[i]) - wave * (u_r[i] - u_l[i]) for i in range(FIELDS)]


def with_flux(u, k):
    f, s = flux(u, primitives(u), k)
    return u, f, s


def iotas():
    sub = lax.broadcasted_iota(jnp.int32, (ROWS, LANES), 0)
    lane = lax.broadcasted_iota(jnp.int32, (ROWS, LANES), 1)
    return sub, lane


def curve_coords(positions, bits):
    coords = [jnp.zeros_like(positions) for _ in range(3)]
    for b in range(bits):
        coords[b % 3] = coords[b % 3] + ((positions >> b) & 1) * 2 ** (b // 3)
    return [c.astype(jnp.float32) for c in coords]


def make_kernel(devices, held):
    npatch = devices * held
    bits = npatch.bit_length() - 1
    strength = GRAV_C / float(npatch) ** (1.0 / 3.0)
    window = held // 2
    low_own, low_far = 0, held
    high_far, high_own = held + window, held + 2 * window

    def kernel(
        state, levels, neighbors, counts,
        ext, grav_out, info_out,
        tin, u0, s1, fin, faces1, faces2, msg, gath, edge_z, edge_y,
        in_sem, out_sem, mass_send, mass_recv, f_send, f_recv, g_send, g_recv,
    ):
        me = lax.axis_index("patch")
        run = lax.axis_index("runs")
        sub, lane = iotas()
        lane_z = lane & (EDGE - 1)
        has_low = me > 0
        has_high = me < devices - 1

        barrier = pltpu.get_barrier_semaphore()

        def greet(i, _):
            pl.semaphore_signal(
                barrier, inc=1, device_id=(run, lax.rem(me + i, devices)),
                device_id_type=pl.DeviceIdType.MESH,
            )
            return 0

        lax.fori_loop(1, devices, greet, 0)
        loads = [
            pltpu.make_async_copy(state.at[f], tin.at[f], in_sem.at[f]) for f in range(FIELDS)
        ]
        for c in loads:
            c.start()
        for c in loads:
            c.wait()

        def plane(ref, p, f, x):
            return ref[p, f, pl.ds(pl.multiple_of(x * ROWS, ROWS), ROWS), :]

        def pack_faces(p, ref, faces):
            for f in range(FIELDS):
                faces[low_own + p, 0, f] = ref[p, f, pl.ds(0, ROWS), :]
                faces[high_own + p, 0, f] = ref[p, f, pl.ds((PLANES - 1) * ROWS, ROWS), :]
                low_y = ref[p, f, pl.ds(0, ROWS, stride=ROWS), :]
                high_y = pltpu.roll(ref[p, f, pl.ds(ROWS - 1, ROWS, stride=ROWS), :], 32, 1)
                for g in range(1, 4):
                    at = g * ROWS * ROWS
                    inside = (lane >> 5) == g
                    more = ref[p, f, pl.ds(at, ROWS, stride=ROWS), :]
                    low_y = jnp.where(inside, pltpu.roll(more, 32 * g, 1), low_y)
                    more = ref[p, f, pl.ds(at + ROWS - 1, ROWS, stride=ROWS), :]
                    high_y = jnp.where(inside, pltpu.roll(more, 32 * (g + 1) % LANES, 1), high_y)
                faces[low_own + p, 1, f] = low_y
                faces[high_own + p, 1, f] = high_y
                low_z = ref[p, f, pl.ds(0, ROWS), :]
                high_z = pltpu.roll(low_z, LANES - 31, 1)
                for x in range(1, PLANES):
                    here = lane_z == x
                    now = ref[p, f, pl.ds(x * ROWS, ROWS), :]
                    low_z = jnp.where(here, pltpu.roll(now, x, 1), low_z)
                    turned = now if x == 31 else pltpu.roll(now, LANES + x - 31, 1)
                    high_z = jnp.where(here, turned, high_z)
                faces[low_own + p, 2, f] = low_z
                faces[high_own + p, 2, f] = high_z

        def unpack(xb, totals):
            totals = list(totals)
            for i in range(2):
                at = pl.ds(pl.multiple_of((xb * 2 + i) * ROWS, ROWS), ROWS)
                for f in range(FIELDS):
                    for p in range(held):
                        v = tin[f, at, p, :]
                        u0[p, f, at, :] = v
                        if f == 0:
                            totals[p] = totals[p] + v
            return tuple(totals)

        zero = jnp.zeros((ROWS, LANES), jnp.float32)
        totals = lax.fori_loop(0, PLANES // 2, unpack, (zero,) * held)

        def pack_first(p, _):
            pack_faces(p, u0, faces1)
            return 0

        lax.fori_loop(0, held, pack_first, 0)
        message = jnp.where(sub == held, counts[0].astype(jnp.float32), 0.0)
        for p in range(held):
            total = jnp.sum(jnp.sum(totals[p], axis=0, keepdims=True), axis=1, keepdims=True)
            level = jnp.full((ROWS, LANES), levels[p].astype(jnp.float32))
            mass = jnp.broadcast_to(total, (ROWS, LANES)) * (1.0 / (LANES * TILES))
            message = jnp.where(sub == p, mass * jnp.exp2(-3.0 * level), message)
        msg[...] = message
        gath[me] = message
        pl.semaphore_wait(barrier, devices - 1)

        def mass_copy(target, slot, s_sem, r_sem):
            return pltpu.make_async_remote_copy(
                src_ref=msg, dst_ref=gath.at[slot], send_sem=s_sem, recv_sem=r_sem,
                device_id=(run, target), device_id_type=pl.DeviceIdType.MESH,
            )

        def face_copies(faces, send, recv):
            down = pltpu.make_async_remote_copy(
                src_ref=faces.at[pl.ds(low_own, window)],
                dst_ref=faces.at[pl.ds(low_far, window)],
                send_sem=send.at[0], recv_sem=recv.at[0],
                device_id=(run, me - 1), device_id_type=pl.DeviceIdType.MESH,
            )
            up = pltpu.make_async_remote_copy(
                src_ref=faces.at[pl.ds(high_own + held - window, window)],
                dst_ref=faces.at[pl.ds(high_far, window)],
                send_sem=send.at[1], recv_sem=recv.at[1],
                device_id=(run, me + 1), device_id_type=pl.DeviceIdType.MESH,
            )
            return down, up

        def start_both(pair):
            pl.when(has_low)(lambda: pair[0].start())
            pl.when(has_high)(lambda: pair[1].start())

        def wait_both(pair):
            pl.when(has_low)(lambda: pair[0].wait_send())
            pl.when(has_high)(lambda: pair[1].wait_send())
            pl.when(has_high)(lambda: pair[0].wait_recv())
            pl.when(has_low)(lambda: pair[1].wait_recv())

        pair1 = face_copies(faces1, f_send.at[0], f_recv.at[0])
        start_both(pair1)

        def send_mass(i, _):
            target = lax.rem(me + i, devices)
            mass_copy(target, me, mass_send.at[i], mass_recv.at[me]).start()
            return 0

        lax.fori_loop(1, devices, send_mass, 0)

        def wait_mass(i, _):
            source = lax.rem(me + i, devices)
            c = mass_copy(source, source, mass_send.at[i], mass_recv.at[source])
            c.wait_send()
            c.wait_recv()
            return 0

        lax.fori_loop(1, devices, wait_mass, 0)

        target = curve_coords(me * held + (lane & (held - 1)), bits)

        def pull(j, sums):
            got_mass = gath[j]
            source = curve_coords(j * held + (sub & (held - 1)), bits)
            off = [source[a] - target[a] for a in range(3)]
            d = off[0] * off[0] + off[1] * off[1] + off[2] * off[2] + SOFTEN
            inv = lax.rsqrt(d)
            w = jnp.where(sub < held, got_mass, 0.0) * (inv * inv * inv)
            is_count = sub == held
            start = sums[3] + jnp.where(is_count & (j < me), got_mass, 0.0)
            count = sums[4] + jnp.where(is_count & (j == me), got_mass, 0.0)
            return tuple(sums[a] + w * off[a] for a in range(3)) + (start, count)

        sums = lax.fori_loop(0, devices, pull, (zero,) * 5)
        sums = [jnp.broadcast_to(jnp.sum(s, axis=0, keepdims=True), (ROWS, LANES)) for s in sums]
        accel = [strength * s for s in sums[:3]]
        grav_out[...] = jnp.where(sub == 0, accel[0], jnp.where(sub == 1, accel[1], accel[2]))
        offset = sums[3].astype(jnp.int32) - me * held + 1
        info_out[...] = jnp.where(lane == 0, offset, sums[4].astype(jnp.int32))

        def advance(p, ref, faces, write):
            level = jnp.full((ROWS, LANES), levels[p].astype(jnp.float32))
            half_ratio = 0.0125 * jnp.exp2(level)
            g = [
                DT_STEP * jnp.broadcast_to(
                    jnp.sum(jnp.where(lane == p, accel[a], 0.0), axis=1, keepdims=True),
                    (ROWS, LANES),
                )
                for a in range(3)
            ]

            def ghost(f, axis):
                nb = neighbors[f, p]
                if f % 2 == 0:
                    slot = jnp.where(nb >= 0, nb - me * held + high_own, low_own + p)
                else:
                    slot = jnp.where(nb >= 0, nb - me * held, high_own + p)
                slot = jnp.clip(slot, 0, 2 * held + 2 * window - 1)
                return [faces[slot, axis, i] for i in range(FIELDS)]

            def own(high, axis):
                base = (high_own if high else low_own) + p
                return [faces[base, axis, i] for i in range(FIELDS)]

            z_low = interface(with_flux(ghost(4, 2), 2), with_flux(own(False, 2), 2))
            z_high = interface(with_flux(own(True, 2), 2), with_flux(ghost(5, 2), 2))
            y_low = interface(with_flux(ghost(2, 1), 1), with_flux(own(False, 1), 1))
            y_high = interface(with_flux(own(True, 1), 1), with_flux(ghost(3, 1), 1))
            for f in range(FIELDS):
                edge_z[0, f] = z_low[f]
                edge_z[1, f] = z_high[f]
                for q in range(4):
                    low = y_low[f] if q == 0 else pltpu.roll(y_low[f], LANES - 32 * q, 1)
                    high = y_high[f] if q == 3 else pltpu.roll(y_high[f], 96 - 32 * q, 1)
                    edge_y[0, f, pl.ds(q * ROWS, ROWS), :] = low
                    edge_y[1, f, pl.ds(q * ROWS, ROWS), :] = high
            before = with_flux(ghost(0, 0), 0)
            pending = [zero] * FIELDS

            at_z0 = lane_z == 0
            at_z31 = lane_z == EDGE - 1
            at_y0 = (sub == 0) & (lane < 32)
            at_y31 = (sub == ROWS - 1) & (lane >= 96)
            carry_low = lane < 32
            carry_high = lane >= 96

            def back_z(v):
                return pltpu.roll(v, 1, 1)

            def ahead_z(v):
                return pltpu.roll(v, LANES - 1, 1)

            def back_y(v):
                t = pltpu.roll(v, 32, 1)
                return jnp.where(carry_low, pltpu.roll(t, 1, 0), t)

            def ahead_y(v):
                t = pltpu.roll(v, LANES - 32, 1)
                return jnp.where(carry_high, pltpu.roll(t, ROWS - 1, 0), t)

            def shifted(u, f, s, k, move):
                mu = [move(v) for v in u]
                mf = [mu[k + 1]] + [move(v) for v in f[1:]]
                return mu, mf, move(s)

            def one(x, before, pending):
                u = [plane(ref, p, f, x) for f in range(FIELDS)]
                prim = primitives(u)
                fx, sx = flux(u, prim, 0)
                gx = interface(before, (u, fx, sx))
                write(p, jnp.maximum(x - 1, 0),
                      [pending[f] - half_ratio * gx[f] for f in range(FIELDS)])
                fy, sy = flux(u, prim, 1)
                gy = interface(shifted(u, fy, sy, 1, back_y), (u, fy, sy))
                fz, sz = flux(u, prim, 2)
                gz = interface(shifted(u, fz, sz, 2, back_z), (u, fz, sz))
                fresh = []
                for f in range(FIELDS):
                    ey0 = edge_y[0, f, pl.ds(x, 1), :]
                    ey1 = edge_y[1, f, pl.ds(x, 1), :]
                    ez0 = pltpu.roll(edge_z[0, f], LANES - x, 1)
                    ez1 = pltpu.roll(edge_z[1, f], LANES + 31 - x, 1)
                    div = jnp.where(at_y31, ey1, ahead_y(gy[f])) - jnp.where(at_y0, ey0, gy[f])
                    div += jnp.where(at_z31, ez1, ahead_z(gz[f])) - jnp.where(at_z0, ez0, gz[f])
                    fresh.append(u[f] - half_ratio * (div - gx[f]))
                for a in range(3):
                    fresh[a + 1] += u[0] * g[a]
                fresh[4] += u[1] * g[0] + u[2] * g[1] + u[3] * g[2]
                return (u, fx, sx), fresh

            def block(xb, carry):
                bu, bf, bs, pend = carry
                before, pend = (list(bu), list(bf), bs), list(pend)
                for i in range(UNROLL):
                    before, pend = one(xb * UNROLL + i, before, pend)
                return tuple(before[0]), tuple(before[1]), before[2], tuple(pend)

            carry = (tuple(before[0]), tuple(before[1]), before[2], tuple(pending))
            bu, bf, bs, pend = lax.fori_loop(0, PLANES // UNROLL, block, carry)
            gx = interface((bu, bf, bs), with_flux(ghost(1, 0), 0))
            write(p, PLANES - 1, [pend[f] - half_ratio * gx[f] for f in range(FIELDS)])

        def rows_of(x):
            return pl.ds(pl.multiple_of(x * ROWS, ROWS), ROWS)

        def write_one(p, x, values):
            for f in range(FIELDS):
                s1[p, f, rows_of(x), :] = values[f]

        def write_two(p, x, values):
            for f in range(FIELDS):
                fin[p, f, rows_of(x), :] = 0.5 * (plane(u0, p, f, x) + values[f])

        wait_both(pair1)

        def stage_one(p, _):
            advance(p, u0, faces1, write_one)
            pack_faces(p, s1, faces2)
            return 0

        lax.fori_loop(0, held, stage_one, 0)
        pair2 = face_copies(faces2, f_send.at[1], f_recv.at[1])
        start_both(pair2)
        wait_both(pair2)

        def patch_copies():
            down = pltpu.make_async_remote_copy(
                src_ref=fin.at[0], dst_ref=ext.at[held + 1],
                send_sem=g_send.at[0], recv_sem=g_recv.at[0],
                device_id=(run, me - 1), device_id_type=pl.DeviceIdType.MESH,
            )
            up = pltpu.make_async_remote_copy(
                src_ref=fin.at[held - 1], dst_ref=ext.at[0],
                send_sem=g_send.at[1], recv_sem=g_recv.at[1],
                device_id=(run, me + 1), device_id_type=pl.DeviceIdType.MESH,
            )
            return down, up

        pair3 = patch_copies()

        def keep(p):
            return pltpu.make_async_copy(fin.at[p], ext.at[p + 1], out_sem.at[p])

        def stage_two(i, _):
            p = lax.rem(i * (held - 1), held)
            advance(p, s1, faces2, write_two)
            keep(p).start()

            @pl.when(i == 1)
            def _():
                start_both(pair3)

            return 0

        lax.fori_loop(0, held, stage_two, 0)
        wait_both(pair3)
        for p in range(held):
            keep(p).wait()

    return kernel


def place_kernel(info, source, out):
    last = source.shape[0] - 1
    offset, count = info[0, 0], info[0, 1]
    for slot in range(CAP):
        used = slot < count
        at = jnp.minimum(slot + offset, last)

        def step(xb, _):
            for i in range(8):
                rows = pl.ds(pl.multiple_of((xb * 8 + i) * ROWS, ROWS), ROWS)
                out[0, rows, slot, :] = jnp.where(used, source[at, 0, rows, :], 0.0)
            return 0

        lax.fori_loop(0, PLANES // 8, step, 0)


def local(state, levels, neighbors, new_counts):
    held = state.shape[0]
    devices = lax.axis_size("patch")
    tiles = state.transpose(1, 0, 2).reshape(FIELDS, held, TILES, LANES).transpose(0, 2, 1, 3)
    f32 = jnp.float32
    smem = pl.BlockSpec(memory_space=pltpu.SMEM)
    vmem = pl.BlockSpec(memory_space=pltpu.VMEM)
    anyspace = pl.BlockSpec(memory_space=pl.ANY)
    dense = (held, FIELDS, TILES, LANES)
    faces = (2 * held + 2 * (held // 2), 3, FIELDS, ROWS, LANES)
    dma = pltpu.SemaphoreType.DMA
    ext, grav, info = pl.pallas_call(
        make_kernel(devices, held),
        out_shape=(
            jax.ShapeDtypeStruct((held + 2, FIELDS, TILES, LANES), f32),
            jax.ShapeDtypeStruct((ROWS, LANES), f32),
            jax.ShapeDtypeStruct((ROWS, LANES), jnp.int32),
        ),
        in_specs=[anyspace, smem, smem, smem],
        out_specs=(anyspace, vmem, vmem),
        scratch_shapes=[
            pltpu.VMEM((FIELDS, TILES, held, LANES), f32),
            pltpu.VMEM(dense, f32),
            pltpu.VMEM(dense, f32),
            pltpu.VMEM(dense, f32),
            pltpu.VMEM(faces, f32),
            pltpu.VMEM(faces, f32),
            pltpu.VMEM((ROWS, LANES), f32),
            pltpu.VMEM((devices, ROWS, LANES), f32),
            pltpu.VMEM((2, FIELDS, ROWS, LANES), f32),
            pltpu.VMEM((2, FIELDS, EDGE, LANES), f32),
            dma((FIELDS,)), dma((held,)),
            dma((devices,)), dma((devices,)),
            dma((2, 2)), dma((2, 2)),
            dma((2,)), dma((2,)),
        ],
        compiler_params=pltpu.CompilerParams(
            collective_id=0, has_side_effects=True, vmem_limit_bytes=48 * 2**20
        ),
        name="advance",
    )(tiles, levels, neighbors, new_counts)
    out = pl.pallas_call(
        place_kernel,
        out_shape=jax.ShapeDtypeStruct((FIELDS, TILES, CAP, LANES), f32),
        grid_spec=pltpu.PrefetchScalarGridSpec(
            num_scalar_prefetch=1,
            grid=(FIELDS,),
            in_specs=[
                pl.BlockSpec(
                    (held + 2, 1, TILES, LANES),
                    lambda f, info: (0, f, 0, 0),
                )
            ],
            out_specs=pl.BlockSpec((1, TILES, CAP, LANES), lambda f, info: (f, 0, 0, 0)),
        ),
        compiler_params=pltpu.CompilerParams(vmem_limit_bytes=60 * 2**20),
        name="place",
    )(info, ext)
    advanced = out.transpose(0, 2, 1, 3).reshape(FIELDS, CAP, TILES * LANES).transpose(1, 0, 2)
    return advanced, grav[:3, :held]


def solution(mesh):
    return jax.shard_map(
        local,
        mesh=mesh,
        in_specs=(
            P(("runs", "patch"), None, None),
            P(("runs", "patch")),
            P(None, ("runs", "patch")),
            P(("runs", "patch")),
        ),
        out_specs=(P(("runs", "patch"), None, None), P(None, ("runs", "patch"))),
        check_vma=False,
    )
```

time: 724 us -> 63.9 us (0.09)
  the two profiles are of different devices: /device:TPU:0 before, /device:TPU:11 now
where the time goes in v1:
time: 63.9 us; the launch traced here: 63.2 us
  Pallas kernels  57.6 us (90%)
  local copies, waits for them, and re-layouts  4.32 us (7%)
  between operations  1.3 us (2%)
    pallas_call x1, Pallas kernels, local(): pl.pallas_call(make_kernel(devices, held), out_shape=(jax.ShapeDtypeStruc...  49.8 us
    pallas_call x1, Pallas kernels, local(): pl.pallas_call(place_kernel, out_shape=jax.ShapeDtypeStruct((FIELDS, TILE...  7.73 us
    unnamed x7, local copies, waits for them, and re-layouts  3.74 us

profile of v1, /device:TPU:11, one launch (start us, length us, event | category | flops | bytes accessed | tf_op | source)
XLA Modules:
  0.0 63.2 jit_solution(5166987064016085724)
XLA Ops:
  1.3 0.8 %copy.6.neighbors = s32[6,4]{1,0:T(8,128)S(1)} copy(s32[6,4]{0,1:T(4,128)} %param.6) | data formatting | bytes 192 | tf_op args[2]
  2.0 0.0 copy-start
  2.0 1.7 %copy-done = f32[4,5,32768]{2,0,1:T(4,128)S(1)} copy-done((f32[4,5,32768]{2,0,1:T(4,128)S(1)}, f32[4,5,32768]{2,0,1:T(4,128)}, u32[]{:S(2)}) %copy-start) | copy-done | bytes 2621464
  3.8 0.0 copy-start.2
  3.8 0.7 %copy-done.2 = s32[4]{0:T(128)S(1)} copy-done((s32[4]{0:T(128)S(1)}, s32[4]{0:T(128)}, u32[]{:S(2)}) %copy-start.2) | copy-done | bytes 40
  4.4 49.8 %advance.1 = (f32[6,5,256,128]{3,2,1,0:T(8,128)}, f32[8,128]{1,0:T(8,128)S(1)}, s32[8,128]{1,0:T(8,128)S(1)}) custom-call(f32[5,256,4,128]{3,2,1,0:T(4,128)S(1)} %bitcast.10, s32[4]{0:T(128)S(1)} %copy-done.2, s32[6,4]{1,0:T(8,128)S(1)} %copy.6.neighbors, s32[1]{0:T(128)S(6)} %copy.7.counts), custom_call_target="tpu_custom_call" | custom-call | tf_op jit(solution)/shard_map/advance/pallas_call | solution.py:429
  54.3 0.0 copy-start.1
  54.3 0.6 copy-done.1
  54.9 0.6 slice.3
  55.5 7.7 %place.1 = f32[5,256,6,128]{3,2,1,0:T(8,128)} custom-call(s32[8,128]{1,0:T(8,128)} %copy-done.1, f32[6,5,256,128]{3,2,1,0:T(8,128)} %get-tuple-element.6.source), custom_call_target="tpu_custom_call" | custom-call | tf_op jit(solution)/shard_map/place/pallas_call | solution.py:459
Async XLA Ops:
  2.0 1.7 %copy-start = (f32[4,5,32768]{2,0,1:T(4,128)S(1)}, f32[4,5,32768]{2,0,1:T(4,128)}, u32[]{:S(2)}) copy-start(f32[4,5,32768]{2,0,1:T(4,128)} %param.4) | copy-start | bytes 7864324
  3.8 0.7 %copy-start.2 = (s32[4]{0:T(128)S(1)}, s32[4]{0:T(128)}, u32[]{:S(2)}) copy-start(s32[4]{0:T(128)} %levels.1) | copy-start | bytes 52
  54.3 0.6 copy-start.1

commit v2 on v1

--- a/solution.py
+++ b/solution.py
@@ -12,6 +12,7 @@
 ROWS = 8
 PLANES = 32
 TILES = 256
+PAD = 8
 
 GAMMA = 1.4
 DT_STEP = 0.01
@@ -73,13 +74,11 @@
     bits = npatch.bit_length() - 1
     strength = GRAV_C / float(npatch) ** (1.0 / 3.0)
     window = held // 2
-    low_own, low_far = 0, held
-    high_far, high_own = held + window, held + 2 * window
 
     def kernel(
         state, levels, neighbors, counts,
         ext, grav_out, info_out,
-        tin, u0, s1, fin, faces1, faces2, msg, gath, edge_z, edge_y,
+        tin, u0, s1, fin, own1, low1, high1, own2, low2, high2, msg, gath, edge_z, edge_y,
         in_sem, out_sem, mass_send, mass_recv, f_send, f_recv, g_send, g_recv,
     ):
         me = lax.axis_index("patch")
@@ -108,41 +107,45 @@
             c.wait()
 
         def plane(ref, p, f, x):
-            return ref[p, f, pl.ds(pl.multiple_of(x * ROWS, ROWS), ROWS), :]
+            return ref[p, f, pl.ds(pl.multiple_of(x * ROWS + PAD, ROWS), ROWS), :]
+
+        def plane_back(ref, p, f, x):
+            return ref[p, f, pl.ds(pl.multiple_of(x * ROWS, ROWS) + (PAD - 1), ROWS), :]
 
         def pack_faces(p, ref, faces):
             for f in range(FIELDS):
-                faces[low_own + p, 0, f] = ref[p, f, pl.ds(0, ROWS), :]
-                faces[high_own + p, 0, f] = ref[p, f, pl.ds((PLANES - 1) * ROWS, ROWS), :]
-                low_y = ref[p, f, pl.ds(0, ROWS, stride=ROWS), :]
-                high_y = pltpu.roll(ref[p, f, pl.ds(ROWS - 1, ROWS, stride=ROWS), :], 32, 1)
+                faces[p, 0, f] = ref[p, f, pl.ds(PAD, ROWS), :]
+                faces[held + p, 0, f] = ref[p, f, pl.ds(PAD + (PLANES - 1) * ROWS, ROWS), :]
+                low_y = ref[p, f, pl.ds(PAD, ROWS, stride=ROWS), :]
+                high_y = pltpu.roll(ref[p, f, pl.ds(PAD + ROWS - 1, ROWS, stride=ROWS), :], 32, 1)
                 for g in range(1, 4):
-                    at = g * ROWS * ROWS
+                    at = PAD + g * ROWS * ROWS
                     inside = (lane >> 5) == g
                     more = ref[p, f, pl.ds(at, ROWS, stride=ROWS), :]
                     low_y = jnp.where(inside, pltpu.roll(more, 32 * g, 1), low_y)
                     more = ref[p, f, pl.ds(at + ROWS - 1, ROWS, stride=ROWS), :]
                     high_y = jnp.where(inside, pltpu.roll(more, 32 * (g + 1) % LANES, 1), high_y)
-                faces[low_own + p, 1, f] = low_y
-                faces[high_own + p, 1, f] = high_y
-                low_z = ref[p, f, pl.ds(0, ROWS), :]
+                faces[p, 1, f] = low_y
+                faces[held + p, 1, f] = high_y
+                low_z = ref[p, f, pl.ds(PAD, ROWS), :]
                 high_z = pltpu.roll(low_z, LANES - 31, 1)
                 for x in range(1, PLANES):
                     here = lane_z == x
-                    now = ref[p, f, pl.ds(x * ROWS, ROWS), :]
+                    now = ref[p, f, pl.ds(PAD + x * ROWS, ROWS), :]
                     low_z = jnp.where(here, pltpu.roll(now, x, 1), low_z)
                     turned = now if x == 31 else pltpu.roll(now, LANES + x - 31, 1)
                     high_z = jnp.where(here, turned, high_z)
-                faces[low_own + p, 2, f] = low_z
-                faces[high_own + p, 2, f] = high_z
+                faces[p, 2, f] = low_z
+                faces[held + p, 2, f] = high_z
 
         def unpack(xb, totals):
             totals = list(totals)
             for i in range(2):
-                at = pl.ds(pl.multiple_of((xb * 2 + i) * ROWS, ROWS), ROWS)
+                x = xb * 2 + i
+                at = pl.ds(pl.multiple_of(x * ROWS + PAD, ROWS), ROWS)
                 for f in range(FIELDS):
                     for p in range(held):
-                        v = tin[f, at, p, :]
+                        v = tin[f, pl.ds(x * (held * ROWS) + p, ROWS, stride=held), :]
                         u0[p, f, at, :] = v
                         if f == 0:
                             totals[p] = totals[p] + v
@@ -152,7 +155,7 @@
         totals = lax.fori_loop(0, PLANES // 2, unpack, (zero,) * held)
 
         def pack_first(p, _):
-            pack_faces(p, u0, faces1)
+            pack_faces(p, u0, own1)
             return 0
 
         lax.fori_loop(0, held, pack_first, 0)
@@ -172,33 +175,38 @@
                 device_id=(run, target), device_id_type=pl.DeviceIdType.MESH,
             )
 
-        def face_copies(faces, send, recv):
+        def face_copies(own, low, high, send, recv):
             down = pltpu.make_async_remote_copy(
-                src_ref=faces.at[pl.ds(low_own, window)],
-                dst_ref=faces.at[pl.ds(low_far, window)],
+                src_ref=own.at[pl.ds(0, window)], dst_ref=high,
                 send_sem=send.at[0], recv_sem=recv.at[0],
                 device_id=(run, me - 1), device_id_type=pl.DeviceIdType.MESH,
             )
             up = pltpu.make_async_remote_copy(
-                src_ref=faces.at[pl.ds(high_own + held - window, window)],
-                dst_ref=faces.at[pl.ds(high_far, window)],
+                src_ref=own.at[pl.ds(2 * held - window, window)], dst_ref=low,
                 send_sem=send.at[1], recv_sem=recv.at[1],
                 device_id=(run, me + 1), device_id_type=pl.DeviceIdType.MESH,
             )
             return down, up
 
-        def start_both(pair):
+        def start_down(pair):
             pl.when(has_low)(lambda: pair[0].start())
+
+        def start_up(pair):
             pl.when(has_high)(lambda: pair[1].start())
 
-        def wait_both(pair):
+        def wait_sent(pair):
             pl.when(has_low)(lambda: pair[0].wait_send())
             pl.when(has_high)(lambda: pair[1].wait_send())
+
+        def wait_from_high(pair):
             pl.when(has_high)(lambda: pair[0].wait_recv())
+
+        def wait_from_low(pair):
             pl.when(has_low)(lambda: pair[1].wait_recv())
 
-        pair1 = face_copies(faces1, f_send.at[0], f_recv.at[0])
-        start_both(pair1)
+        pair1 = face_copies(own1, low1, high1, f_send.at[0], f_recv.at[0])
+        start_down(pair1)
+        start_up(pair1)
 
         def send_mass(i, _):
             target = lax.rem(me + i, devices)
@@ -237,7 +245,7 @@
         offset = sums[3].astype(jnp.int32) - me * held + 1
         info_out[...] = jnp.where(lane == 0, offset, sums[4].astype(jnp.int32))
 
-        def advance(p, ref, faces, write):
+        def advance(p, ref, own_faces, far, from_low, write):
             level = jnp.full((ROWS, LANES), levels[p].astype(jnp.float32))
             half_ratio = 0.0125 * jnp.exp2(level)
             g = [
@@ -249,25 +257,32 @@
             ]
 
             def ghost(f, axis):
-                nb = neighbors[f, p]
-                if f % 2 == 0:
-                    slot = jnp.where(nb >= 0, nb - me * held + high_own, low_own + p)
-                else:
-                    slot = jnp.where(nb >= 0, nb - me * held, high_own + p)
-                slot = jnp.clip(slot, 0, 2 * held + 2 * window - 1)
-                return [faces[slot, axis, i] for i in range(FIELDS)]
+                nb = neighbors[p, f]
+                base = held * (1 - f % 2)
+                near = jnp.where(nb >= 0, base + jnp.clip(nb - me * held, 0, held - 1),
+                                 held * (f % 2) + p)
+                out = [own_faces[near, axis, i] for i in range(FIELDS)]
+                if from_low == (f % 2 == 0):
+                    if from_low:
+                        slot, away = nb - me * held + window, (nb >= 0) & (nb < me * held)
+                    else:
+                        slot, away = nb - (me + 1) * held, nb >= (me + 1) * held
+                    slot = jnp.clip(slot, 0, window - 1)
+                    out = [jnp.where(away, far[slot, axis, i], out[i]) for i in range(FIELDS)]
+                return out
 
             def own(high, axis):
-                base = (high_own if high else low_own) + p
-                return [faces[base, axis, i] for i in range(FIELDS)]
+                base = held * int(high) + p
+                return [own_faces[base, axis, i] for i in range(FIELDS)]
 
             z_low = interface(with_flux(ghost(4, 2), 2), with_flux(own(False, 2), 2))
             z_high = interface(with_flux(own(True, 2), 2), with_flux(ghost(5, 2), 2))
             y_low = interface(with_flux(ghost(2, 1), 1), with_flux(own(False, 1), 1))
             y_high = interface(with_flux(own(True, 1), 1), with_flux(ghost(3, 1), 1))
             for f in range(FIELDS):
-                edge_z[0, f] = z_low[f]
-                edge_z[1, f] = z_high[f]
+                turned = pltpu.roll(z_high[f], EDGE - 1, 1)
+                edge_z[0, f] = jnp.where((lane & 1) == 0, z_low[f], turned)
+                edge_z[1, f] = jnp.where((lane & 1) == 1, z_low[f], turned)
                 for q in range(4):
                     low = y_low[f] if q == 0 else pltpu.roll(y_low[f], LANES - 32 * q, 1)
                     high = y_high[f] if q == 3 else pltpu.roll(y_high[f], 96 - 32 * q, 1)
@@ -280,7 +295,6 @@
             at_z31 = lane_z == EDGE - 1
             at_y0 = (sub == 0) & (lane < 32)
             at_y31 = (sub == ROWS - 1) & (lane >= 96)
-            carry_low = lane < 32
             carry_high = lane >= 96
 
             def back_z(v):
@@ -288,10 +302,6 @@
 
             def ahead_z(v):
                 return pltpu.roll(v, LANES - 1, 1)
-
-            def back_y(v):
-                t = pltpu.roll(v, 32, 1)
-                return jnp.where(carry_low, pltpu.roll(t, 1, 0), t)
 
             def ahead_y(v):
                 t = pltpu.roll(v, LANES - 32, 1)
@@ -302,7 +312,7 @@
                 mf = [mu[k + 1]] + [move(v) for v in f[1:]]
                 return mu, mf, move(s)
 
-            def one(x, before, pending):
+            def one(x, odd, before, pending):
                 u = [plane(ref, p, f, x) for f in range(FIELDS)]
                 prim = primitives(u)
                 fx, sx = flux(u, prim, 0)
@@ -310,17 +320,18 @@
                 write(p, jnp.maximum(x - 1, 0),
                       [pending[f] - half_ratio * gx[f] for f in range(FIELDS)])
                 fy, sy = flux(u, prim, 1)
-                gy = interface(shifted(u, fy, sy, 1, back_y), (u, fy, sy))
+                rows = [plane_back(ref, p, f, x) for f in range(FIELDS)]
+                below = [pltpu.roll(jnp.where(carry_high, rows[f], u[f]), 32, 1) for f in range(FIELDS)]
+                gy = interface(with_flux(below, 1), (u, fy, sy))
                 fz, sz = flux(u, prim, 2)
                 gz = interface(shifted(u, fz, sz, 2, back_z), (u, fz, sz))
                 fresh = []
                 for f in range(FIELDS):
                     ey0 = edge_y[0, f, pl.ds(x, 1), :]
                     ey1 = edge_y[1, f, pl.ds(x, 1), :]
-                    ez0 = pltpu.roll(edge_z[0, f], LANES - x, 1)
-                    ez1 = pltpu.roll(edge_z[1, f], LANES + 31 - x, 1)
+                    ez = pltpu.roll(edge_z[odd, f], LANES - x, 1)
                     div = jnp.where(at_y31, ey1, ahead_y(gy[f])) - jnp.where(at_y0, ey0, gy[f])
-                    div += jnp.where(at_z31, ez1, ahead_z(gz[f])) - jnp.where(at_z0, ez0, gz[f])
+                    div += jnp.where(at_z31, ez, ahead_z(gz[f])) - jnp.where(at_z0, ez, gz[f])
                     fresh.append(u[f] - half_ratio * (div - gx[f]))
                 for a in range(3):
                     fresh[a + 1] += u[0] * g[a]
@@ -331,7 +342,7 @@
                 bu, bf, bs, pend = carry
                 before, pend = (list(bu), list(bf), bs), list(pend)
                 for i in range(UNROLL):
-                    before, pend = one(xb * UNROLL + i, before, pend)
+                    before, pend = one(xb * UNROLL + i, i % 2, before, pend)
                 return tuple(before[0]), tuple(before[1]), before[2], tuple(pend)
 
             carry = (tuple(before[0]), tuple(before[1]), before[2], tuple(pending))
@@ -344,23 +355,28 @@
 
         def write_one(p, x, values):
             for f in range(FIELDS):
-                s1[p, f, rows_of(x), :] = values[f]
+                s1[p, f, pl.ds(pl.multiple_of(x * ROWS + PAD, ROWS), ROWS), :] = values[f]
 
         def write_two(p, x, values):
             for f in range(FIELDS):
                 fin[p, f, rows_of(x), :] = 0.5 * (plane(u0, p, f, x) + values[f])
 
-        wait_both(pair1)
-
-        def stage_one(p, _):
-            advance(p, u0, faces1, write_one)
-            pack_faces(p, s1, faces2)
-            return 0
-
-        lax.fori_loop(0, held, stage_one, 0)
-        pair2 = face_copies(faces2, f_send.at[1], f_recv.at[1])
-        start_both(pair2)
-        wait_both(pair2)
+        wait_from_low(pair1)
+        wait_from_high(pair1)
+        pair2 = face_copies(own2, low2, high2, f_send.at[1], f_recv.at[1])
+
+        def stage_one(far, from_low):
+            def step(p, _):
+                advance(p, u0, own1, far, from_low, write_one)
+                pack_faces(p, s1, own2)
+                return 0
+
+            return step
+
+        lax.fori_loop(0, window, stage_one(low1, True), 0)
+        start_down(pair2)
+        lax.fori_loop(window, held, stage_one(high1, False), 0)
+        start_up(pair2)
 
         def patch_copies():
             down = pltpu.make_async_remote_copy(
@@ -380,51 +396,71 @@
         def keep(p):
             return pltpu.make_async_copy(fin.at[p], ext.at[p + 1], out_sem.at[p])
 
-        def stage_two(i, _):
-            p = lax.rem(i * (held - 1), held)
-            advance(p, s1, faces2, write_two)
+        def stage_two(p, far, from_low):
+            advance(p, s1, own2, far, from_low, write_two)
             keep(p).start()
 
-            @pl.when(i == 1)
-            def _():
-                start_both(pair3)
-
+        wait_from_high(pair2)
+        stage_two(held - 1, high2, False)
+        start_up(pair3)
+        wait_from_low(pair2)
+        stage_two(0, low2, True)
+        start_down(pair3)
+
+        def inner_high(i, _):
+            stage_two(i, high2, False)
             return 0
 
-        lax.fori_loop(0, held, stage_two, 0)
-        wait_both(pair3)
+        def inner_low(i, _):
+            stage_two(i, low2, True)
+            return 0
+
+        lax.fori_loop(window, held - 1, inner_high, 0)
+        lax.fori_loop(1, window, inner_low, 0)
+        for pair in (pair1, pair2, pair3):
+            wait_sent(pair)
+        wait_from_low(pair3)
+        wait_from_high(pair3)
         for p in range(held):
             keep(p).wait()
 
     return kernel
 
 
-def place_kernel(info, source, out):
+def place_kernel(info, source, grav, out, grav_out):
     last = source.shape[0] - 1
     offset, count = info[0, 0], info[0, 1]
-    for slot in range(CAP):
-        used = slot < count
-        at = jnp.minimum(slot + offset, last)
-
-        def step(xb, _):
-            for i in range(8):
-                rows = pl.ds(pl.multiple_of((xb * 8 + i) * ROWS, ROWS), ROWS)
-                out[0, rows, slot, :] = jnp.where(used, source[at, 0, rows, :], 0.0)
-            return 0
-
-        lax.fori_loop(0, PLANES // 8, step, 0)
+    sub, _ = iotas()
+    used = sub < count
+    at = [jnp.minimum(slot + offset, last) for slot in range(CAP)]
+
+    def step(rb, _):
+        for i in range(16):
+            row = rb * 16 + i
+            tile = jnp.zeros((ROWS, LANES), jnp.float32)
+            for slot in range(CAP):
+                line = jnp.broadcast_to(source[at[slot], 0, pl.ds(row, 1), :], (ROWS, LANES))
+                tile = line if slot == 0 else jnp.where(sub == slot, line, tile)
+            out[0, row] = jnp.where(used, tile, 0.0)[:CAP]
+        return 0
+
+    lax.fori_loop(0, TILES // 16, step, 0)
+    grav_out[...] = grav[: grav_out.shape[0], : grav_out.shape[1]]
 
 
 def local(state, levels, neighbors, new_counts):
     held = state.shape[0]
     devices = lax.axis_size("patch")
     tiles = state.transpose(1, 0, 2).reshape(FIELDS, held, TILES, LANES).transpose(0, 2, 1, 3)
+    tiles = tiles.reshape(FIELDS, TILES * held, LANES)
     f32 = jnp.float32
     smem = pl.BlockSpec(memory_space=pltpu.SMEM)
     vmem = pl.BlockSpec(memory_space=pltpu.VMEM)
     anyspace = pl.BlockSpec(memory_space=pl.ANY)
+    padded = (held, FIELDS, TILES + PAD, LANES)
     dense = (held, FIELDS, TILES, LANES)
-    faces = (2 * held + 2 * (held // 2), 3, FIELDS, ROWS, LANES)
+    faces = (2 * held, 3, FIELDS, ROWS, LANES)
+    far = (held // 2,) + faces[1:]
     dma = pltpu.SemaphoreType.DMA
     ext, grav, info = pl.pallas_call(
         make_kernel(devices, held),
@@ -436,12 +472,12 @@
         in_specs=[anyspace, smem, smem, smem],
         out_specs=(anyspace, vmem, vmem),
         scratch_shapes=[
-            pltpu.VMEM((FIELDS, TILES, held, LANES), f32),
+            pltpu.VMEM((FIELDS, TILES * held, LANES), f32),
+            pltpu.VMEM(padded, f32),
+            pltpu.VMEM(padded, f32),
             pltpu.VMEM(dense, f32),
-            pltpu.VMEM(dense, f32),
-            pltpu.VMEM(dense, f32),
-            pltpu.VMEM(faces, f32),
-            pltpu.VMEM(faces, f32),
+            pltpu.VMEM(faces, f32), pltpu.VMEM(far, f32), pltpu.VMEM(far, f32),
+            pltpu.VMEM(faces, f32), pltpu.VMEM(far, f32), pltpu.VMEM(far, f32),
             pltpu.VMEM((ROWS, LANES), f32),
             pltpu.VMEM((devices, ROWS, LANES), f32),
             pltpu.VMEM((2, FIELDS, ROWS, LANES), f32),
@@ -452,13 +488,16 @@
             dma((2,)), dma((2,)),
         ],
         compiler_params=pltpu.CompilerParams(
-            collective_id=0, has_side_effects=True, vmem_limit_bytes=48 * 2**20
+            collective_id=0, has_side_effects=True, vmem_limit_bytes=60 * 2**20
         ),
         name="advance",
-    )(tiles, levels, neighbors, new_counts)
-    out = pl.pallas_call(
+    )(tiles, levels, neighbors.T, new_counts)
+    out, gravity = pl.pallas_call(
         place_kernel,
-        out_shape=jax.ShapeDtypeStruct((FIELDS, TILES, CAP, LANES), f32),
+        out_shape=(
+            jax.ShapeDtypeStruct((FIELDS, TILES, CAP, LANES), f32),
+            jax.ShapeDtypeStruct((3, held), f32),
+        ),
         grid_spec=pltpu.PrefetchScalarGridSpec(
             num_scalar_prefetch=1,
             grid=(FIELDS,),
@@ -466,15 +505,19 @@
                 pl.BlockSpec(
                     (held + 2, 1, TILES, LANES),
                     lambda f, info: (0, f, 0, 0),
-                )
+                ),
+                pl.BlockSpec((ROWS, LANES), lambda f, info: (0, 0)),
             ],
-            out_specs=pl.BlockSpec((1, TILES, CAP, LANES), lambda f, info: (f, 0, 0, 0)),
+            out_specs=(
+                pl.BlockSpec((1, TILES, CAP, LANES), lambda f, info: (f, 0, 0, 0)),
+                pl.BlockSpec((3, held), lambda f, info: (0, 0)),
+            ),
         ),
         compiler_params=pltpu.CompilerParams(vmem_limit_bytes=60 * 2**20),
         name="place",
-    )(info, ext)
+    )(info, ext, grav)
     advanced = out.transpose(0, 2, 1, 3).reshape(FIELDS, CAP, TILES * LANES).transpose(1, 0, 2)
-    return advanced, grav[:3, :held]
+    return advanced, gravity
 
 
 def solution(mesh):

time: 63.9 us -> 51.1 us (0.80)
  Pallas kernels: 57.6 us -> 49.4 us
  local copies, waits for them, and re-layouts: 4.32 us -> 0 us
    pallas_call x1, Pallas kernels: 49.8 us -> 41.8 us  [local(): pl.pallas_call(make_kernel(devices, held), out_shape=(jax.ShapeDtypeStruc...]
    unnamed x7 -> x0, local copies, waits for them, and re-layouts: 3.74 us -> none
where the time goes in v2:
time: 51.1 us; the launch traced here: 50.7 us
  Pallas kernels  49.4 us (97%)
  between operations  1.28 us (3%)
    pallas_call x1, Pallas kernels, local(): pl.pallas_call(make_kernel(devices, held), out_shape=(jax.ShapeDtypeStruc...  41.8 us
    pallas_call x1, Pallas kernels, local(): pl.pallas_call(place_kernel, out_shape=(jax.ShapeDtypeStruct((FIELDS, TIL...  7.65 us

profile of v2, /device:TPU:11, one launch (start us, length us, event | category | flops | bytes accessed | tf_op | source)
XLA Modules:
  0.0 50.7 jit_solution(4592367877002303065)
XLA Ops:
  1.3 41.8 %advance.1 = (f32[6,5,256,128]{3,2,1,0:T(8,128)}, f32[8,128]{1,0:T(8,128)}, s32[8,128]{1,0:T(8,128)}) custom-call(f32[5,1024,128]{2,1,0:T(8,128)} %bitcast.13, s32[4]{0:T(128)} %levels.1, s32[4,6]{1,0:T(4,128)} %bitcast.14, s32[1]{0:T(128)S(6)} %copy.7.counts), custom_call_target="tpu_custom_call" | custom-call | tf_op jit(solution)/shard_map/advance/pallas_call | solution.py:465
  43.1 7.6 %place.1 = (f32[5,256,6,128]{3,2,1,0:T(8,128)}, f32[3,4]{1,0:T(4,128)}) custom-call(s32[8,128]{1,0:T(8,128)} %get-tuple-element.7.info, f32[6,5,256,128]{3,2,1,0:T(8,128)} %get-tuple-element.8.source, f32[8,128]{1,0:T(8,128)} %get-tuple-element.9.grav), custom_call_target="tpu_custom_call" | custom-call | tf_op jit(solution)/shard_map/place/pallas_call | solution.py:495

commit v3 on v2

--- a/solution.py
+++ b/solution.py
@@ -88,6 +88,12 @@
         has_low = me > 0
         has_high = me < devices - 1
 
+        loads = [
+            pltpu.make_async_copy(state.at[f], tin.at[f], in_sem.at[f]) for f in range(FIELDS)
+        ]
+        for c in loads:
+            c.start()
+
         barrier = pltpu.get_barrier_semaphore()
 
         def greet(i, _):
@@ -98,14 +104,6 @@
             return 0
 
         lax.fori_loop(1, devices, greet, 0)
-        loads = [
-            pltpu.make_async_copy(state.at[f], tin.at[f], in_sem.at[f]) for f in range(FIELDS)
-        ]
-        for c in loads:
-            c.start()
-        for c in loads:
-            c.wait()
-
         def plane(ref, p, f, x):
             return ref[p, f, pl.ds(pl.multiple_of(x * ROWS + PAD, ROWS), ROWS), :]
 
@@ -138,27 +136,24 @@
                 faces[p, 2, f] = low_z
                 faces[held + p, 2, f] = high_z
 
-        def unpack(xb, totals):
-            totals = list(totals)
-            for i in range(2):
-                x = xb * 2 + i
-                at = pl.ds(pl.multiple_of(x * ROWS + PAD, ROWS), ROWS)
-                for f in range(FIELDS):
+        def unpack(f):
+            def step(xb, totals):
+                totals = list(totals)
+                for i in range(8):
+                    x = xb * 8 + i
+                    at = pl.ds(pl.multiple_of(x * ROWS + PAD, ROWS), ROWS)
                     for p in range(held):
                         v = tin[f, pl.ds(x * (held * ROWS) + p, ROWS, stride=held), :]
                         u0[p, f, at, :] = v
                         if f == 0:
                             totals[p] = totals[p] + v
-            return tuple(totals)
+                return tuple(totals)
+
+            loads[f].wait()
+            return lax.fori_loop(0, PLANES // 8, step, (zero,) * held if f == 0 else ())
 
         zero = jnp.zeros((ROWS, LANES), jnp.float32)
-        totals = lax.fori_loop(0, PLANES // 2, unpack, (zero,) * held)
-
-        def pack_first(p, _):
-            pack_faces(p, u0, own1)
-            return 0
-
-        lax.fori_loop(0, held, pack_first, 0)
+        totals = unpack(0)
         message = jnp.where(sub == held, counts[0].astype(jnp.float32), 0.0)
         for p in range(held):
             total = jnp.sum(jnp.sum(totals[p], axis=0, keepdims=True), axis=1, keepdims=True)
@@ -204,16 +199,23 @@
         def wait_from_low(pair):
             pl.when(has_low)(lambda: pair[1].wait_recv())
 
-        pair1 = face_copies(own1, low1, high1, f_send.at[0], f_recv.at[0])
-        start_down(pair1)
-        start_up(pair1)
-
         def send_mass(i, _):
             target = lax.rem(me + i, devices)
             mass_copy(target, me, mass_send.at[i], mass_recv.at[me]).start()
             return 0
 
         lax.fori_loop(1, devices, send_mass, 0)
+        for f in range(1, FIELDS):
+            unpack(f)
+
+        def pack_first(p, _):
+            pack_faces(p, u0, own1)
+            return 0
+
+        lax.fori_loop(0, held, pack_first, 0)
+        pair1 = face_copies(own1, low1, high1, f_send.at[0], f_recv.at[0])
+        start_down(pair1)
+        start_up(pair1)
 
         def wait_mass(i, _):
             source = lax.rem(me + i, devices)
@@ -238,11 +240,18 @@
             count = sums[4] + jnp.where(is_count & (j == me), got_mass, 0.0)
             return tuple(sums[a] + w * off[a] for a in range(3)) + (start, count)
 
-        sums = lax.fori_loop(0, devices, pull, (zero,) * 5)
+        group = 4 if devices % 4 == 0 else 1
+
+        def pull_group(jb, sums):
+            for i in range(group):
+                sums = pull(jb * group + i, sums)
+            return sums
+
+        sums = lax.fori_loop(0, devices // group, pull_group, (zero,) * 5)
         sums = [jnp.broadcast_to(jnp.sum(s, axis=0, keepdims=True), (ROWS, LANES)) for s in sums]
         accel = [strength * s for s in sums[:3]]
         grav_out[...] = jnp.where(sub == 0, accel[0], jnp.where(sub == 1, accel[1], accel[2]))
-        offset = sums[3].astype(jnp.int32) - me * held + 1
+        offset = jnp.clip(sums[3].astype(jnp.int32) - me * held + 1, 0, CAP - held)
         info_out[...] = jnp.where(lane == 0, offset, sums[4].astype(jnp.int32))
 
         def advance(p, ref, own_faces, far, from_low, write):
@@ -444,7 +453,7 @@
             out[0, row] = jnp.where(used, tile, 0.0)[:CAP]
         return 0
 
-    lax.fori_loop(0, TILES // 16, step, 0)
+    lax.fori_loop(0, out.shape[1] // 16, step, 0)
     grav_out[...] = grav[: grav_out.shape[0], : grav_out.shape[1]]
 
 
@@ -500,17 +509,17 @@
         ),
         grid_spec=pltpu.PrefetchScalarGridSpec(
             num_scalar_prefetch=1,
-            grid=(FIELDS,),
+            grid=(FIELDS, 2),
             in_specs=[
                 pl.BlockSpec(
-                    (held + 2, 1, TILES, LANES),
-                    lambda f, info: (0, f, 0, 0),
+                    (held + 2, 1, TILES // 2, LANES),
+                    lambda f, h, info: (0, f, h, 0),
                 ),
-                pl.BlockSpec((ROWS, LANES), lambda f, info: (0, 0)),
+                pl.BlockSpec((ROWS, LANES), lambda f, h, info: (0, 0)),
             ],
             out_specs=(
-                pl.BlockSpec((1, TILES, CAP, LANES), lambda f, info: (f, 0, 0, 0)),
-                pl.BlockSpec((3, held), lambda f, info: (0, 0)),
+                pl.BlockSpec((1, TILES // 2, CAP, LANES), lambda f, h, info: (f, h, 0, 0)),
+                pl.BlockSpec((3, held), lambda f, h, info: (0, 0)),
             ),
         ),
         compiler_params=pltpu.CompilerParams(vmem_limit_bytes=60 * 2**20),

time: 51.1 us -> 51.5 us (level)
    pallas_call x1, Pallas kernels: 7.65 us -> 9.23 us  [local(): pl.pallas_call(place_kernel, out_shape=(jax.ShapeDtypeStruct((FIELDS, TIL...]
    pallas_call x1, Pallas kernels: 41.8 us -> 40.6 us  [local(): pl.pallas_call(make_kernel(devices, held), out_shape=(jax.ShapeDtypeStruc...]
where the time goes in v3:
time: 51.5 us; the launch traced here: 51.1 us
  Pallas kernels  49.8 us (97%)
  between operations  1.28 us (2%)
    pallas_call x1, Pallas kernels, local(): pl.pallas_call(make_kernel(devices, held), out_shape=(jax.ShapeDtypeStruc...  40.6 us
    pallas_call x1, Pallas kernels, local(): pl.pallas_call(place_kernel, out_shape=(jax.ShapeDtypeStruct((FIELDS, TIL...  9.23 us

profile of v3, /device:TPU:11, one launch (start us, length us, event | category | flops | bytes accessed | tf_op | source)
XLA Modules:
  0.0 51.1 jit_solution(15027336504285672827)
XLA Ops:
  1.3 40.6 %advance.1 = (f32[6,5,256,128]{3,2,1,0:T(8,128)}, f32[8,128]{1,0:T(8,128)}, s32[8,128]{1,0:T(8,128)}) custom-call(f32[5,1024,128]{2,1,0:T(8,128)} %bitcast.13, s32[4]{0:T(128)} %levels.1, s32[4,6]{1,0:T(4,128)} %bitcast.14, s32[1]{0:T(128)S(6)} %copy.7.counts), custom_call_target="tpu_custom_call" | custom-call | tf_op jit(solution)/shard_map/advance/pallas_call | solution.py:474
  41.9 9.2 %place.1 = (f32[5,256,6,128]{3,2,1,0:T(8,128)}, f32[3,4]{1,0:T(4,128)}) custom-call(s32[8,128]{1,0:T(8,128)} %get-tuple-element.7.info, f32[6,5,256,128]{3,2,1,0:T(8,128)} %get-tuple-element.8.source, f32[8,128]{1,0:T(8,128)} %get-tuple-element.9.grav), custom_call_target="tpu_custom_call" | custom-call | tf_op jit(solution)/shard_map/place/pallas_call | solution.py:504
